TPU v7x, 32 devices: a whole 2x2x4 slice. The times are simulated.
32 devices in a mesh: tok: 8 (over z, x), head: 4 (over y, core).
Axes of the slice: x: 2, y: 2, z: 4, core: 2. Of those that a mesh axis runs over, the one named last changes fastest.
Arguments:
- embeddings: bfloat16 [1024, 4096], P('tok'), may hold values from -6 to 6
- norm_gain: bfloat16 [4096], replicated, may hold values from 0.099609375 to 1.8984375
- query_key_value_weight: bfloat16 [4096, 6144], P(None, 'head'), may hold values from -0.09375 to 0.09375
- embed_table: bfloat16 [65536, 4096], P('tok', 'head'), may hold values from -6 to 6
- rotated_cache_pages: bfloat16 [8, 8, 256, 2048], P('tok', None, None, 'head'), may hold values from -300 to 300
- page_owner_device: int32 [8, 8], P('tok'), may hold values from 0 to 7, each once within a row
- cached_length: int32 [8], P('tok'), may hold values from 2 to 2048, as said below
- vocab_shard: int32 [1024, 1], P('tok'), may hold values from 0 to 7; in each aligned block of 128 rows (0 to 127, 128 to 255, ...) at most 32 rows name the same one
- shard_row: int32 [1024], P('tok'), may hold values from 0 to 8191
- accept: int32 [1024], P('tok'), may hold values from 0 to 1, as said below
Outputs:
- out_first: bfloat16 [1024, 4096], P('tok', 'head')
- out_second: bfloat16 [1024, 4096], P('tok', 'head')
Inputs may be any that keep to these rules, and one draw needn't show every extreme that they name: `page_owner_device`: each row names every device of the tok axis once. `cached_length`: some request has exactly 2048 cached positions. `vocab_shard`: at most 32 of the 128 tokens of one request name the same shard, and some shard is named that often. `accept`: at most 32 accepted tokens in one request's block; some block has exactly 32.
All inputs are finite; a program needn't handle non-finite values.
Results may differ from a plain program's by a relative error of at most 0.017.
The roundings to bfloat16 on the way count: a program that leaves them out, or rounds other values in their place, can miss the bound.
Values may be sent and summed in bfloat16 or wider, within the bound.
A program may use at most 128 MiB of HBM per device.

v0:
```python
import math

import jax
import jax.numpy as jnp
from jax import lax
from jax.sharding import PartitionSpec as P

QUERY_HEADS = 32
KEY_VALUE_HEADS = 8
HEAD_SIZE = 128


THETA = 500000.0


def angles(positions):
    steps_half = jnp.arange(HEAD_SIZE // 2, dtype=jnp.float32)
    frequency = THETA ** (-(steps_half * 2.0) / HEAD_SIZE)
    return positions.astype(jnp.float32)[:, None] * frequency[None, :]


def rotate(vectors, turning):
    half_width = vectors.shape[-1] // 2
    former = vectors[..., :half_width]
    latter = vectors[..., half_width:]
    cosine = jnp.cos(turning)
    sine_of = jnp.sin(turning)
    return jnp.concatenate(
        [former * cosine - latter * sine_of, latter * cosine + former * sine_of], axis=-1
    )


def project(inputs, norm_gain, query_key_value_weight, positions):
    widened = inputs.astype(jnp.float32)
    inverse = lax.rsqrt(jnp.mean(widened * widened, axis=-1, keepdims=True) + 1e-05)
    normed = (widened * inverse * norm_gain.astype(jnp.float32)).astype(jnp.bfloat16)
    combined = jnp.dot(normed, query_key_value_weight, preferred_element_type=jnp.float32)
    heads_per_group = QUERY_HEADS // KEY_VALUE_HEADS
    combined = combined.reshape(inputs.shape[0], -1, heads_per_group + 2, HEAD_SIZE)
    turning = angles(positions)[:, None, None, :]
    query_vectors = rotate(combined[:, :, :heads_per_group], turning).astype(jnp.bfloat16)
    block_keys = rotate(combined[:, :, heads_per_group : heads_per_group + 1], turning)[
        :, :, 0
    ].astype(jnp.bfloat16)
    block_values = combined[:, :, heads_per_group + 1].astype(jnp.bfloat16)
    return (query_vectors, block_keys, block_values)


def attend(query_vectors, block_keys, block_values, page_keys, page_values, usable):
    factor = 1.0 / math.sqrt(HEAD_SIZE)
    scores_cache = (
        jnp.einsum("bgqd,kgd->gqbk", query_vectors, page_keys, preferred_element_type=jnp.float32)
        * factor
    )
    scores_cache = jnp.where(usable[None, None, None, :], scores_cache, -1e30)
    scores_block = (
        jnp.einsum("bgqd,cgd->gqbc", query_vectors, block_keys, preferred_element_type=jnp.float32)
        * factor
    )
    highest = jnp.maximum(jnp.max(scores_cache, axis=-1), jnp.max(scores_block, axis=-1))[..., None]
    exp_cache = jnp.exp(scores_cache - highest)
    exp_block = jnp.exp(scores_block - highest)
    totals = jnp.sum(exp_cache, axis=-1) + jnp.sum(exp_block, axis=-1)
    weights_cache = exp_cache.astype(jnp.bfloat16)
    weights_block = exp_block.astype(jnp.bfloat16)
    combined = jnp.einsum(
        "gqbk,kgd->bgqd", weights_cache, page_values, preferred_element_type=jnp.float32
    )
    combined = combined + jnp.einsum(
        "gqbc,cgd->bgqd", weights_block, block_values, preferred_element_type=jnp.float32
    )
    result = combined / jnp.transpose(totals, (2, 0, 1))[..., None]
    return result.astype(jnp.bfloat16).reshape(query_vectors.shape[0], -1)


def body(
    embeddings,
    norm_gain,
    query_key_value_weight,
    embed_table,
    rotated_cache_pages,
    page_owner_device,
    cached_length,
    vocab_shard,
    shard_row,
    accept,
):
    members = lax.axis_size("tok")
    length = embeddings.shape[0]
    sources = jnp.arange(members, dtype=jnp.int32)
    positions = cached_length[0] + jnp.arange(length, dtype=jnp.int32)
    query_vectors, block_keys, block_values = project(
        embeddings, norm_gain, query_key_value_weight, positions
    )
    arrived = lax.all_to_all(rotated_cache_pages, "tok", split_axis=1, concat_axis=0, tiled=True)
    page_size = arrived.shape[2]
    arrived = arrived.reshape(members * page_size, -1, 2, HEAD_SIZE)
    page_index = jnp.sum(
        jnp.where(page_owner_device[0][:, None] == sources[None, :], sources[:, None], 0), axis=0
    )
    page_spots = page_index[:, None] * page_size + jnp.arange(page_size, dtype=jnp.int32)[None, :]
    usable = page_spots.reshape(-1) < cached_length[0]
    page_keys = arrived[:, :, 0]
    page_values = arrived[:, :, 1]

    def run_attention(query_rows, key_rows, value_rows):
        return attend(query_rows, key_rows, value_rows, page_keys, page_values, usable)

    output_one = run_attention(query_vectors, block_keys, block_values)
    target_shard = vocab_shard[:, 0]
    capacity = max(2, 2 * length // members)
    chosen = (target_shard[:, None] == sources[None, :]).astype(jnp.int32)
    earlier = (jnp.arange(length)[:, None] > jnp.arange(length)[None, :]).astype(jnp.int32)
    slot_rank = jnp.sum(jnp.dot(earlier, chosen) * chosen, axis=1)
    wanted = jnp.zeros((members, capacity), jnp.int32).at[target_shard, slot_rank].set(shard_row)
    found_rows = jnp.take(
        embed_table, lax.all_to_all(wanted, "tok", split_axis=0, concat_axis=0, tiled=True), axis=0
    )
    returned = lax.all_to_all(found_rows, "tok", split_axis=0, concat_axis=0, tiled=True)
    replacement = returned[target_shard, slot_rank]
    full_rows = lax.all_gather(replacement, "head", axis=1, tiled=True)
    replaced = jnp.where(accept[:, None] == 1, full_rows, embeddings)
    queries_two, keys_two, values_two = project(
        replaced, norm_gain, query_key_value_weight, positions
    )
    output_two = run_attention(queries_two, keys_two, values_two)
    return (output_one, output_two)


def solution(mesh):
    return jax.shard_map(
        body,
        mesh=mesh,
        in_specs=(
            P("tok", None),
            P(),
            P(None, "head"),
            P("tok", "head"),
            P("tok", None, None, "head"),
            P("tok", None),
            P("tok"),
            P("tok", None),
            P("tok"),
            P("tok"),
        ),
        out_specs=(P("tok", "head"), P("tok", "head")),
        check_vma=False,
    )
```

profile of v0, /device:TPU:0, one launch (start us, length us, event | category | flops | bytes accessed | tf_op | source)
XLA Modules:
  0.0 149.1 jit_solution(12598932373189895741)
XLA Ops:
  7.2 0.9 fusion.32
  8.2 0.7 fusion.63
  8.8 11.0 %scatter_fusion = s32[8,32]{1,0:T(8,128)S(1)} fusion(s32[8,32]{1,0:T(8,128)S(1)} %broadcast_in_dim.55, s32[128]{0:T(128)S(1)} %get-tuple-element.16, s32[128]{0:T(128)} %param.18), kind=kCustom, calls=%fused_computation.2 | custom fusion | bytes 2560 | tf_op jit(solution)/shard_map/scatter | solution.py:115
  19.8 13.5 %all_to_all.29 = s32[8,1,32]{2,1,0:T(1,128)S(1)} all-to-all(s32[8,1,32]{2,1,0:T(1,128)S(1)} %bitcast.132), channel_id=1, replica_groups=mesh['tok'=8,'head'=4] {'tok'}, dimensions={0} | all-to-all | bytes 2048 | tf_op jit(solution)/shard_map/all_to_all | solution.py:117
  33.4 9.5 %gather_fusion = bf16[256,1024]{1,0:T(8,128)(2,1)S(1)} fusion(bf16[8192,1024]{1,0:T(8,128)(2,1)} %param.13, s32[1024]{0:T(1024)S(1)} %pad_clamp_fusion), kind=kCustom, calls=%fused_computation | custom fusion | bytes 1049600 | tf_op jit(solution)/shard_map/jit(_take)/gather | solution.py:116
  43.1 15.7 %all_to_all.30 = bf16[8,32,1024]{2,1,0:T(8,128)(2,1)S(1)} all-to-all(bf16[8,32,1024]{2,1,0:T(8,128)(2,1)S(1)} %broadcast_select_fusion.1), channel_id=1, replica_groups=mesh['tok'=8,'head'=4] {'tok'}, dimensions={0} | all-to-all | bytes 1048576 | tf_op jit(solution)/shard_map/all_to_all | solution.py:119
  58.8 2.4 %gather_fusion.1 = bf16[128,1024]{1,0:T(8,128)(2,1)} fusion(bf16[8,32,1024]{2,1,0:T(8,128)(2,1)S(1)} %all_to_all.30, s32[128]{0:T(128)S(1)} %bitcast.133), kind=kCustom, calls=%fused_computation.1 | custom fusion | bytes 525312 | tf_op jit(solution)/shard_map/gather | solution.py:120
  61.2 4.5 %all-to-all-start = ((bf16[1,8,256,512]{3,2,0,1:T(8,128)(2,1)}), bf16[1,8,256,512]{3,2,0,1:T(8,128)(2,1)}, u32[]{:S(2)}, u32[]{:S(2)}) async-start(bf16[1,8,256,512]{3,2,0,1:T(8,128)(2,1)} %bitcast.140), calls=%async_computation | async-start | bytes 4194304 | tf_op jit(solution)/shard_map/all_to_all | solution.py:95
  66.6 0.3 multiply_cosine_fusion
  66.9 10.2 %all-gather.2.cloned.1.call-done = bf16[128,4096]{1,0:T(8,128)(2,1)} async-done(((bf16[128,1024]{1,0:T(8,128)(2,1)}), bf16[128,4096]{1,0:T(8,128)(2,1)}) %all-gather.2.cloned.1.call-update) | async-done | bytes 1048592 | tf_op jit(solution)/shard_map/all_gather | solution.py:121
  77.1 1.9 %fusion.15 = (f32[128]{0:T(128)S(1)}, f32[128]{0:T(128)S(1)}) fusion(bf16[128,4096]{1,0:T(8,128)(2,1)} %all-gather.2.cloned.1.call-done, bf16[128,4096]{1,0:T(8,128)(2,1)S(1)} %copy-done, pred[128]{0:T(512)(128)(4,1)S(1)} %broadcast_compare_fusion), kind=kLoop, calls=%fused_computation.26 | loop fusion | flops 3669760 | bytes 2098304 | tf_op jit(solution)/shard_map/reduce_sum | solution.py:35
  79.0 8.4 %fusion.33 = f32[128,1536]{0,1:T(8,128)S(1)} fusion(bf16[4096,1536]{1,0:T(8,128)(2,1)} %param.12, f32[128]{0:T(128)S(1)} %get-tuple-element.47, f32[4096]{0:T(1024)S(1)} %convert_element_type.63, bf16[128,4096]{1,0:T(8,128)(2,1)} %all-gather.2.cloned.1.call-done, bf16[128,4096]{1,0:T(8,128)(2,1)S(1)} %copy-done, pred[128]{0:T(512)(128)(4,1)S(1)} %broadcast_compare_fusion), kind=kOutput, calls=%fused_computation.45 | convolution fusion | flops 1613234176 | bytes 15483520 | tf_op jit(solution)/shard_map/dot_general | solution.py:37
  87.7 1.0 copy.105
  88.7 1.0 copy.104
  89.7 8.0 %fusion.35 = f32[128,1536]{0,1:T(8,128)S(1)} fusion(bf16[4096,1536]{1,0:T(8,128)(2,1)} %param.12, bf16[128,4096]{1,0:T(8,128)(2,1)S(1)} %copy-done, f32[4096]{0:T(1024)S(1)} %convert_element_type.63, f32[128]{0:T(128)S(1)} %get-tuple-element.48), kind=kOutput, calls=%fused_computation.46 | convolution fusion | flops 1612709888 | bytes 14434816 | tf_op jit(solution)/shard_map/dot_general | solution.py:37
  98.0 0.2 copy.99
  98.5 1.5 subtract_convert_fusion
  100.0 1.1 fusion.79
  101.2 1.1 fusion.78
  102.3 10.4 %all-to-all-done = bf16[1,8,256,512]{3,2,0,1:T(8,128)(2,1)} async-done(((bf16[1,8,256,512]{3,2,0,1:T(8,128)(2,1)}), bf16[1,8,256,512]{3,2,0,1:T(8,128)(2,1)}, u32[]{:S(2)}, u32[]{:S(2)}) %all-to-all-start) | async-done | bytes 2097184 | tf_op jit(solution)/shard_map/all_to_all | solution.py:95
  112.7 2.5 %reshape.214 = bf16[2048,2,2,128]{3,2,1,0:T(2,128)(2,1)S(1)} reshape(bf16[1,8,256,512]{3,2,0,1:T(8,128)(2,1)} %all-to-all-done) | data formatting | bytes 4194304 | tf_op jit(solution)/shard_map/reshape | solution.py:97
  115.2 4.2 %fusion.73 = (bf16[2048,2,1,128]{3,2,1,0:T(2,128)(2,1)}, bf16[2048,2,1,128]{3,2,1,0:T(2,128)(2,1)}) fusion(bf16[2048,2,2,128]{3,2,1,0:T(2,128)(2,1)S(1)} %reshape.214), kind=kLoop, calls=%fused_computation.121 | loop fusion | bytes 4194304 | tf_op jit(solution)/shard_map/slice | solution.py:104
  119.4 6.0 %copy.103 = bf16[2048,2,1,128]{0,3,1,2:T(8,128)(2,1)} copy(bf16[2048,2,1,128]{3,2,1,0:T(2,128)(2,1)} %get-tuple-element.18) | data formatting | bytes 2097152
  125.4 3.1 %fusion.48 = f32[2,128,4,2048]{3,1,2,0:T(8,128)S(1)} fusion(bf16[2048,2,1,128]{3,2,1,0:T(2,128)(2,1)} %get-tuple-element.19, bf16[128,2,4,64]{3,0,2,1:T(8,128)(2,1)} %copy-done.3, bf16[128,2,4,64]{3,0,2,1:T(8,128)(2,1)} %copy-done.4), kind=kOutput, calls=%fused_computation.67 | convolution fusion | flops 537395200 | bytes 9699328 | tf_op jit(solution)/shard_map/bgqd,kgd->gqbk/dot_general | solution.py:52
  128.5 2.6 %bitcast_reduce_fusion = (f32[2,4,128]{2,1,0:T(4,128)S(1)}, f32[2,4,128]{2,1,0:T(4,128)S(1)}, f32[2,128,4,2048]{3,1,2,0:T(8,128)S(1)}) fusion(pred[2048]{0:T(1024)(128)(4,1)S(1)} %lt.48, f32[2,128,4,2048]{3,1,2,0:T(8,128)S(1)} %fusion.48, bf16[2048,2,1,128]{3,2,1,0:T(2,128)(2,1)S(1)} %copy-done.1, bf16[128,2,4,64]{3,0,2,1:T(8,128)(2,1)S(1)} %get-tuple-element.21, ...), kind=kOutput, calls=%fused_computation.4 | convolution fusion | flops 549976064 | bytes 18098176 | tf_op jit(solution)/shard_map/bgqd,kgd->gqbk/dot_general | solution.py:52
  131.2 2.1 %fusion.18 = f32[128,2,4,128]{0,3,2,1:T(8,128)S(1)} fusion(f32[2,128,4,2048]{3,1,2,0:T(8,128)S(1)} %fusion.48, f32[2,4,128]{2,1,0:T(4,128)S(1)} %max.14, pred[2048]{0:T(1024)(128)(4,1)S(1)} %lt.48, bf16[2048,2,1,128]{0,3,1,2:T(8,128)(2,1)S(1)} %copy-done.7), kind=kOutput, calls=%fused_computation.29 | convolution fusion | flops 545259520 | bytes 9967616 | tf_op jit(solution)/shard_map/gqbk,kgd->bgqd/dot_general | solution.py:66
  133.2 3.6 %fusion.4 = (f32[2,4,128]{2,1,0:T(4,128)S(1)}, f32[2,4,128]{2,1,0:T(4,128)S(1)}) fusion(f32[2,128,4,2048]{3,1,2,0:T(8,128)S(1)} %get-tuple-element.42, f32[2,4,128]{2,1,0:T(4,128)S(1)} %max.15, pred[2048]{0:T(1024)(128)(4,1)S(1)} %lt.48, f32[2,4,128]{2,1,0:T(4,128)S(1)} %max.14, f32[2,128,4,2048]{3,1,2,0:T(8,128)S(1)} %fusion.48), kind=kLoop, calls=%fused_computation.13 | loop fusion | flops 16775168 | bytes 16795648 | tf_op jit(solution)/shard_map/reduce_sum | solution.py:63
  136.8 2.0 %fusion.21 = f32[128,2,4,128]{0,3,2,1:T(8,128)S(1)} fusion(f32[2,128,4,2048]{3,1,2,0:T(8,128)S(1)} %get-tuple-element.42, f32[2,4,128]{2,1,0:T(4,128)S(1)} %max.15, pred[2048]{0:T(1024)(128)(4,1)S(1)} %lt.48, bf16[2048,2,1,128]{0,3,1,2:T(8,128)(2,1)S(1)} %copy-done.7), kind=kOutput, calls=%fused_computation.30 | convolution fusion | flops 545259520 | bytes 9967616 | tf_op jit(solution)/shard_map/gqbk,kgd->bgqd/dot_general | solution.py:66
  139.1 0.2 fusion.30
  139.4 0.9 copy.84
  140.2 1.2 fusion.31
  141.4 0.9 copy.83
  (55 shorter events, 1.5 us)
Async XLA Ops:
  7.2 59.2 %copy-start.9 = (s32[1,8]{1,0:T(1,128)S(1)}, s32[1,8]{1,0:T(1,128)}, u32[]{:S(2)}) copy-start(s32[1,8]{1,0:T(1,128)} %param.15) | copy-start | bytes 100
  7.2 59.4 %copy-start.8 = (bf16[4096]{0:T(1024)(128)(2,1)S(1)}, bf16[4096]{0:T(1024)(128)(2,1)}, u32[]{:S(2)}) copy-start(bf16[4096]{0:T(1024)(128)(2,1)} %param.11) | copy-start | bytes 24580
  7.2 59.4 %copy-start.10 = (s32[128]{0:T(128)S(1)}, s32[128]{0:T(128)}, u32[]{:S(2)}) copy-start(s32[128]{0:T(128)} %param.19) | copy-start | bytes 1540
  7.2 69.9 %copy-start = (bf16[128,4096]{1,0:T(8,128)(2,1)S(1)}, bf16[128,4096]{1,0:T(8,128)(2,1)}, u32[]{:S(2)}) copy-start(bf16[128,4096]{1,0:T(8,128)(2,1)} %param.10) | copy-start | bytes 3145732
  7.2 69.9 %all-gather.2.cloned.1.call-start = ((), (), s32[]{:S(2)}) async-start(), calls=%async_computation.3 | async-start | bytes 1310720 | tf_op jit(solution)/shard_map/all_gather | solution.py:121
  61.2 51.5 %all-to-all-start = ((bf16[1,8,256,512]{3,2,0,1:T(8,128)(2,1)}), bf16[1,8,256,512]{3,2,0,1:T(8,128)(2,1)}, u32[]{:S(2)}, u32[]{:S(2)}) async-start(bf16[1,8,256,512]{3,2,0,1:T(8,128)(2,1)} %bitcast.140), calls=%async_computation | async-start | bytes 4194304 | tf_op jit(solution)/shard_map/all_to_all | solution.py:95
  97.7 4.6 %copy-start.2 = (f32[128,1536]{0,1:T(8,128)}, f32[128,1536]{0,1:T(8,128)S(1)}, u32[]{:S(2)}) copy-start(f32[128,1536]{0,1:T(8,128)S(1)} %fusion.35) | copy-start | bytes 2359300
  100.0 1.2 copy-start.4
  100.0 2.3 %copy-start.3 = (bf16[128,2,4,64]{3,0,2,1:T(8,128)(2,1)}, bf16[128,2,4,64]{3,0,2,1:T(8,128)(2,1)S(1)}, u32[]{:S(2)}) copy-start(bf16[128,2,4,64]{3,0,2,1:T(8,128)(2,1)S(1)} %get-tuple-element.38) | copy-start | bytes 393220
  119.4 9.0 %copy-start.1 = (bf16[2048,2,1,128]{3,2,1,0:T(2,128)(2,1)S(1)}, bf16[2048,2,1,128]{3,2,1,0:T(2,128)(2,1)}, u32[]{:S(2)}) copy-start(bf16[2048,2,1,128]{3,2,1,0:T(2,128)(2,1)} %get-tuple-element.19) | copy-start | bytes 3145732
  128.5 2.7 %copy-start.7 = (bf16[2048,2,1,128]{0,3,1,2:T(8,128)(2,1)S(1)}, bf16[2048,2,1,128]{0,3,1,2:T(8,128)(2,1)}, u32[]{:S(2)}) copy-start(bf16[2048,2,1,128]{0,3,1,2:T(8,128)(2,1)} %copy.103) | copy-start | bytes 3145732
  136.8 2.1 %copy-start.5 = (f32[2,4,128,128]{2,3,1,0:T(8,128)S(1)}, f32[2,4,128,128]{2,3,1,0:T(8,128)}, u32[]{:S(2)}) copy-start(f32[2,4,128,128]{2,3,1,0:T(8,128)} %get-tuple-element.44) | copy-start | bytes 1572868
  136.8 2.2 %copy-start.6 = (f32[2,4,128,128]{2,3,1,0:T(8,128)S(1)}, f32[2,4,128,128]{2,3,1,0:T(8,128)}, u32[]{:S(2)}) copy-start(f32[2,4,128,128]{2,3,1,0:T(8,128)} %get-tuple-element.46) | copy-start | bytes 1572868
Sparse Core Ops, SparseCore 0:
  61.3 15.7 all-gather.1
where the time goes:
time: 150 us; the launch traced here: 149 us
  local copies, waits for them, and re-layouts  40.3 us (27%)
  matrix products  30.8 us (21%)
  blocking collectives  29.3 us (20%)
  waiting for transfers between devices  20.6 us (14%)
  between operations  15.1 us (10%)
  other arithmetic  8.5 us (6%)
  starting transfers between devices  4.57 us (3%)
    dot_general x2, matrix products, project(): jnp.dot(normed, query_key_value_weight, preferred_element_type=jnp.float32)  16.4 us
    all_to_all x1, blocking collectives, body(): lax.all_to_all(found_rows, 'tok', split_axis=0, concat_axis=0, tiled=True)  15.7 us
    all_to_all x1, blocking collectives, body(): lax.all_to_all(wanted, 'tok', split_axis=0, concat_axis=0, tiled=True)  13.5 us
    scatter x1, local copies, waits for them, and re-layouts, body(): jnp.zeros((members, capacity), jnp.int32).at[target_shard, slot_rank]  11 us
    unnamed x33, local copies, waits for them, and re-layouts  10.5 us
    all_to_all x1, waiting for transfers between devices, body(): lax.all_to_all(rotated_cache_pages, 'tok', split_axis=1, concat_axis=0, t...  10.4 us
    all_gather x1, waiting for transfers between devices, body(): full_rows = lax.all_gather(replacement, 'head', axis=1, tiled=True)  10.2 us
    gather x1, local copies, waits for them, and re-layouts, body(): jnp.take(embed_table, lax.all_to_all(wanted, 'tok', split_axis=0, concat_...  9.48 us
  transfers between devices with their start and end apart: 2, of which 2 were waited for; matrix products, arithmetic and copies ran while one was open for 17% of the time, Pallas kernels for 0%

commit v1 on v0

v1 whole, which is shorter than its diff:
```python
import functools
import math

import jax
import jax.numpy as jnp
from jax import lax
from jax.experimental import pallas as pl
from jax.experimental.pallas import tpu as pltpu
from jax.sharding import PartitionSpec as P

QUERY_HEADS = 32
KEY_VALUE_HEADS = 8
HEAD_SIZE = 128
HEADS_PER_GROUP = QUERY_HEADS // KEY_VALUE_HEADS
ACCEPTED = 32
THETA = 500000.0
MASKED = -1e30
SCALE = math.log2(math.e) / math.sqrt(HEAD_SIZE)
MESH = pl.DeviceIdType.MESH


def kernel(
    members, heads, inner,
    page_ref, length_ref, emb_ref, gain_ref, cos_ref, sin_ref, ids_ref, sel_ref, accept_ref,
    w_hbm, table_hbm, pages_hbm,
    out1_ref, out2_ref,
    w, table, pages, x2, normed, q, kb, vb, top, total, acc,
    ids_all, found_acc, found, recv_a, sum_a, recv_b, rows,
    w_sem, table_sem, own_sem, page_send, page_recv, ids_send, ids_recv,
    a_send, a_recv, b_send, b_recv, h_send, h_recv,
):
    me = lax.axis_index("tok")
    my_head = lax.axis_index("head")
    outer = members // inner
    my_outer, my_inner = me // inner, lax.rem(me, inner)
    groups = w.shape[1] // ((HEADS_PER_GROUP + 2) * HEAD_SIZE)
    length = emb_ref.shape[0]
    slots, width = found.shape[2], found.shape[3]
    page_size = pages.shape[1]
    q_rows = HEADS_PER_GROUP * length

    def tok_peer(step):
        return lax.rem(me + step, members)

    def tok_source(step):
        return lax.rem(me - step + members, members)

    def page_copy(step):
        peer = tok_peer(step)
        return pltpu.make_async_remote_copy(
            src_ref=pages_hbm.at[0, peer], dst_ref=pages.at[me],
            send_sem=page_send.at[peer], recv_sem=page_recv.at[me],
            device_id={"tok": peer}, device_id_type=MESH,
        )

    def page_arrival(source):
        return pltpu.make_async_remote_copy(
            src_ref=pages_hbm.at[0, source], dst_ref=pages.at[source],
            send_sem=page_send.at[source], recv_sem=page_recv.at[source],
            device_id={"tok": source}, device_id_type=MESH,
        )

    def ids_copy(peer, slot):
        return pltpu.make_async_remote_copy(
            src_ref=ids_ref, dst_ref=ids_all.at[slot],
            send_sem=ids_send.at[peer], recv_sem=ids_recv.at[slot],
            device_id={"tok": peer}, device_id_type=MESH,
        )

    def a_copy(other, slot):
        return pltpu.make_async_remote_copy(
            src_ref=found.at[:, other], dst_ref=recv_a.at[slot],
            send_sem=a_send.at[other], recv_sem=a_recv.at[slot],
            device_id={"tok": my_outer * inner + other}, device_id_type=MESH,
        )

    def b_copy(other, slot):
        return pltpu.make_async_remote_copy(
            src_ref=sum_a.at[other], dst_ref=recv_b.at[slot],
            send_sem=b_send.at[other], recv_sem=b_recv.at[slot],
            device_id={"tok": other * inner + my_inner}, device_id_type=MESH,
        )

    def h_copy(other, slot):
        return pltpu.make_async_remote_copy(
            src_ref=rows.at[my_head], dst_ref=rows.at[slot],
            send_sem=h_send.at[other], recv_sem=h_recv.at[slot],
            device_id={"head": other}, device_id_type=MESH,
        )

    table_chunk = table.shape[0] // table_sem.shape[0]

    def table_copy(i):
        part = pl.ds(pl.multiple_of(i * table_chunk, table_chunk), table_chunk)
        return pltpu.make_async_copy(table_hbm.at[part], table.at[part], table_sem.at[i])

    def w_copy(i):
        part = pl.ds(i * 2 * HEAD_SIZE, 2 * HEAD_SIZE)
        return pltpu.make_async_copy(w_hbm.at[:, part], w.at[:, part], w_sem.at[i])

    own_copy = pltpu.make_async_copy(pages_hbm.at[0, me], pages.at[me], own_sem)

    @pl.loop(0, table_sem.shape[0])
    def _(i):
        table_copy(i).start()

    barrier = pltpu.get_barrier_semaphore()

    @pl.loop(1, members)
    def _(step):
        pl.semaphore_signal(
            barrier, inc=1, device_id={"tok": tok_peer(step)}, device_id_type=MESH
        )

    @pl.loop(1, heads)
    def _(step):
        pl.semaphore_signal(
            barrier, inc=1, device_id={"head": lax.rem(my_head + step, heads)},
            device_id_type=MESH,
        )

    pl.semaphore_wait(barrier, members - 1 + heads - 1)

    @pl.loop(1, members)
    def _(step):
        ids_copy(tok_peer(step), me).start()

    @pl.loop(1, members)
    def _(step):
        page_copy(step).start()

    for i in range(3 * groups):
        w_copy(i).start()
    own_copy.start()
    ids_all[me] = ids_ref[...]

    def normalize(x_ref):
        @pl.loop(0, length // 16)
        def _(i):
            part = pl.ds(pl.multiple_of(i * 16, 16), 16)
            x = x_ref[part, :].astype(jnp.float32)
            inverse = lax.rsqrt(jnp.mean(x * x, axis=-1, keepdims=True) + 1e-05)
            normed[part, :] = (x * inverse * gain_ref[...].astype(jnp.float32)).astype(jnp.bfloat16)

    def rotated(v):
        return (v * cos_ref[...] + pltpu.roll(v, HEAD_SIZE // 2, 1) * sin_ref[...]).astype(
            jnp.bfloat16
        )

    def project(p):
        for g in range(groups):
            for c in range(3):
                i = g * 3 + c
                if p == 0:
                    w_copy(i).wait()
                y = jnp.dot(
                    normed[...], w[:, i * 256 : (i + 1) * 256], preferred_element_type=jnp.float32
                )
                left, right = y[:, :HEAD_SIZE], y[:, HEAD_SIZE:]
                if c < 2:
                    row = 2 * c * length
                    q[p, g, row : row + length, :] = rotated(left)
                    q[p, g, row + length : row + 2 * length, :] = rotated(right)
                else:
                    kb[p, g] = rotated(left)
                    vb[p, g] = right.astype(jnp.bfloat16)

    def scores_of(keys, p, g):
        return SCALE * lax.dot_general(
            keys, q[p, g], (((1,), (1,)), ((), ())), preferred_element_type=jnp.float32
        )

    def weighted(values, weights):
        return lax.dot_general(
            values, weights.astype(jnp.bfloat16), (((0,), (0,)), ((), ())),
            preferred_element_type=jnp.float32,
        )

    def attend_block(p):
        for g in range(groups):
            s = scores_of(kb[p, g], p, g)
            high = jnp.max(s, axis=0, keepdims=True)
            e = jnp.exp2(s - high)
            top[p, g] = high
            total[p, g] = jnp.sum(e, axis=0, keepdims=True)
            acc[p, g] = weighted(vb[p, g], e)

    def attend_page(source, p):
        limit = length_ref[0] - page_ref[0, source] * page_size
        usable = lax.broadcasted_iota(jnp.int32, (page_size, q_rows), 0) < limit
        for g in range(groups):
            keys = pages[source, :, g * 256 : g * 256 + 128]
            values = pages[source, :, g * 256 + 128 : g * 256 + 256]
            s = jnp.where(usable, scores_of(keys, p, g), MASKED)
            before = top[p, g]
            high = jnp.maximum(before, jnp.max(s, axis=0, keepdims=True))
            shrink = jnp.exp2(before - high)
            e = jnp.exp2(s - high)
            top[p, g] = high
            total[p, g] = total[p, g] * shrink + jnp.sum(e, axis=0, keepdims=True)
            acc[p, g] = acc[p, g] * shrink + weighted(values, e)

    normalize(emb_ref)

    @pl.loop(1, members)
    def _(step):
        source = tok_source(step)
        ids_copy(source, source).wait_recv()

    found_acc[...] = jnp.zeros_like(found_acc)
    wanted = ids_all[...].reshape(members * slots, HEAD_SIZE)[:, :1] - me * table.shape[0]

    @pl.loop(0, table_sem.shape[0])
    def _(i):
        table_copy(i).wait()
        spots = lax.broadcasted_iota(jnp.int32, (members * slots, table_chunk), 1)
        hot = jnp.where(wanted - i * table_chunk == spots, 1.0, 0.0).astype(jnp.bfloat16)
        part = pl.ds(pl.multiple_of(i * table_chunk, table_chunk), table_chunk)
        found_acc[...] += jnp.dot(hot, table[part, :], preferred_element_type=jnp.float32)

    for m in range(members):
        found[m // inner, m % inner] = found_acc[m * slots : (m + 1) * slots, :].astype(jnp.bfloat16)

    @pl.loop(1, inner)
    def _(step):
        a_copy(lax.rem(my_inner + step, inner), my_inner).start()

    project(0)

    sum_a[...] = found[:, my_inner]

    @pl.loop(1, inner)
    def _(step):
        source = lax.rem(my_inner - step + inner, inner)
        a_copy(source, source).wait_recv()
        sum_a[...] += recv_a[source]

    @pl.loop(1, outer)
    def _(step):
        b_copy(lax.rem(my_outer + step, outer), my_outer).start()

    attend_block(0)
    rows[my_head] = sum_a[my_outer]

    @pl.loop(1, outer)
    def _(step):
        source = lax.rem(my_outer - step + outer, outer)
        b_copy(source, source).wait_recv()
        rows[my_head] += recv_b[source]

    @pl.loop(1, heads)
    def _(step):
        h_copy(lax.rem(my_head + step, heads), my_head).start()

    own_copy.wait()
    attend_page(me, 0)

    @pl.loop(1, heads)
    def _(step):
        source = lax.rem(my_head - step + heads, heads)
        h_copy(source, source).wait_recv()

    for h in range(heads):
        part = slice(h * width, (h + 1) * width)
        placed = jnp.dot(sel_ref[...], rows[h], preferred_element_type=jnp.float32)
        x2[:, part] = jnp.where(
            accept_ref[...] == 1, placed, emb_ref[:, part].astype(jnp.float32)
        ).astype(jnp.bfloat16)
    normalize(x2)
    project(1)
    attend_block(1)
    attend_page(me, 1)

    @pl.loop(1, members)
    def _(step):
        source = tok_source(step)
        page_arrival(source).wait_recv()
        attend_page(source, 0)
        attend_page(source, 1)

    for p, out in enumerate((out1_ref, out2_ref)):
        for g in range(groups):
            result = acc[p, g] / total[p, g]
            for h in range(HEADS_PER_GROUP):
                column = (g * HEADS_PER_GROUP + h) * HEAD_SIZE
                out[:, column : column + HEAD_SIZE] = result[
                    :, h * length : (h + 1) * length
                ].T.astype(jnp.bfloat16)

    @pl.loop(1, members)
    def _(step):
        ids_copy(tok_peer(step), me).wait_send()
        page_copy(step).wait_send()

    @pl.loop(1, inner)
    def _(step):
        a_copy(lax.rem(my_inner + step, inner), my_inner).wait_send()

    @pl.loop(1, outer)
    def _(step):
        b_copy(lax.rem(my_outer + step, outer), my_outer).wait_send()

    @pl.loop(1, heads)
    def _(step):
        h_copy(lax.rem(my_head + step, heads), my_head).wait_send()


def body(
    embeddings, norm_gain, query_key_value_weight, embed_table, rotated_cache_pages,
    page_owner_device, cached_length, vocab_shard, shard_row, accept,
):
    members = lax.axis_size("tok")
    heads = lax.axis_size("head")
    inner = 1
    while 4 * inner * inner <= members:
        inner *= 2
    outer = members // inner
    length, model = embeddings.shape
    columns = query_key_value_weight.shape[1]
    shard_rows, width = embed_table.shape
    page_size = rotated_cache_pages.shape[2]
    groups = columns // ((HEADS_PER_GROUP + 2) * HEAD_SIZE)
    slots = ACCEPTED
    q_rows = HEADS_PER_GROUP * length

    positions = (cached_length[0] + jnp.arange(length, dtype=jnp.int32)).astype(jnp.float32)
    halves = jnp.arange(HEAD_SIZE, dtype=jnp.int32) % (HEAD_SIZE // 2)
    frequency = THETA ** (-(halves.astype(jnp.float32) * 2.0) / HEAD_SIZE)
    turning = positions[:, None] * frequency[None, :]
    sign = jnp.where(jnp.arange(HEAD_SIZE) < HEAD_SIZE // 2, -1.0, 1.0)
    cosine, sine = jnp.cos(turning), jnp.sin(turning) * sign[None, :]

    sources = jnp.arange(members, dtype=jnp.int32)
    page_index = jnp.sum(
        jnp.where(page_owner_device[0][:, None] == sources[None, :], sources[:, None], 0), axis=0
    )[None, :]
    token_ids = vocab_shard[:, 0] * shard_rows + shard_row
    order = jnp.arange(length)
    earlier = jnp.sum(
        jnp.where(order[None, :] < order[:, None], accept[None, :], 0), axis=1
    )
    selected = (accept[:, None] == 1) & (earlier[:, None] == jnp.arange(slots)[None, :])
    slot_ids = jnp.sum(jnp.where(selected, token_ids[:, None], 0), axis=0)
    slot_ids = jnp.broadcast_to(slot_ids[:, None], (slots, 128)).astype(jnp.int32)

    vmem = pl.BlockSpec(memory_space=pltpu.VMEM)
    smem = pl.BlockSpec(memory_space=pltpu.SMEM)
    anywhere = pl.BlockSpec(memory_space=pl.ANY)
    bf16, f32 = jnp.bfloat16, jnp.float32
    table_chunks = max(1, shard_rows // 1024)
    dma = pltpu.SemaphoreType.DMA
    return pl.pallas_call(
        functools.partial(kernel, members, heads, inner),
        out_shape=(
            jax.ShapeDtypeStruct((length, groups * q_rows), bf16),
            jax.ShapeDtypeStruct((length, groups * q_rows), bf16),
        ),
        in_specs=[smem, smem] + [vmem] * 7 + [anywhere] * 3,
        out_specs=(vmem, vmem),
        scratch_shapes=[
            pltpu.VMEM((model, columns), bf16),
            pltpu.VMEM((shard_rows, width), bf16),
            pltpu.VMEM((members, page_size, rotated_cache_pages.shape[3]), bf16),
            pltpu.VMEM((length, model), bf16),
            pltpu.VMEM((length, model), bf16),
            pltpu.VMEM((2, groups, q_rows, HEAD_SIZE), bf16),
            pltpu.VMEM((2, groups, length, HEAD_SIZE), bf16),
            pltpu.VMEM((2, groups, length, HEAD_SIZE), bf16),
            pltpu.VMEM((2, groups, 1, q_rows), f32),
            pltpu.VMEM((2, groups, 1, q_rows), f32),
            pltpu.VMEM((2, groups, HEAD_SIZE, q_rows), f32),
            pltpu.VMEM((members, slots, 128), jnp.int32),
            pltpu.VMEM((members * slots, width), f32),
            pltpu.VMEM((outer, inner, slots, width), bf16),
            pltpu.VMEM((inner, outer, slots, width), bf16),
            pltpu.VMEM((outer, slots, width), bf16),
            pltpu.VMEM((outer, slots, width), bf16),
            pltpu.VMEM((heads, slots, width), bf16),
            dma((3 * groups,)),
            dma((table_chunks,)),
            dma,
            dma((members,)), dma((members,)), dma((members,)), dma((members,)),
            dma((inner,)), dma((inner,)), dma((outer,)), dma((outer,)),
            dma((heads,)), dma((heads,)),
        ],
        compiler_params=pltpu.CompilerParams(
            collective_id=0, has_side_effects=True, vmem_limit_bytes=56 * 2**20
        ),
    )(
        page_index, cached_length, embeddings, norm_gain[None, :], cosine, sine, slot_ids,
        selected.astype(bf16), accept[:, None],
        query_key_value_weight, embed_table, rotated_cache_pages,
    )


def solution(mesh):
    return jax.shard_map(
        body,
        mesh=mesh,
        in_specs=(
            P("tok", None),
            P(),
            P(None, "head"),
            P("tok", "head"),
            P("tok", None, None, "head"),
            P("tok", None),
            P("tok"),
            P("tok", None),
            P("tok"),
            P("tok"),
        ),
        out_specs=(P("tok", "head"), P("tok", "head")),
        check_vma=False,
    )
```

time: 150 us -> 94.8 us (0.63)
  Pallas kernels: 0 us -> 81.3 us
  local copies, waits for them, and re-layouts: 40.3 us -> 6.69 us
  matrix products: 30.8 us -> 0 us
  blocking collectives: 29.3 us -> 0 us
  waiting for transfers between devices: 20.6 us -> 0 us
  between operations: 15.1 us -> 1.31 us
  starting transfers between devices: 4.57 us -> 0 us
  other arithmetic: 8.5 us -> 5.17 us
    pallas_call x0 -> x1, Pallas kernels: none -> 81.3 us  [body(): pl.pallas_call(functools.partial(kernel, members, heads, inner), out_shap...]
    dot_general x11 -> x0, matrix products: 30.8 us -> none  [the longest x2 16.4 us: project(): jnp.dot(normed, query_key_value_weight, preferred_element_type=jnp.float32)]
    all_to_all x2 -> x0, blocking collectives: 29.3 us -> none  [the longest x1 15.7 us: body(): lax.all_to_all(found_rows, 'tok', split_axis=0, concat_axis=0, tiled=True)]
    gather x2 -> x0, local copies, waits for them, and re-layouts: 11.8 us -> none  [the longest x1 9.48 us: body(): jnp.take(embed_table, lax.all_to_all(wanted, 'tok', split_axis=0, concat_...]
    scatter x1 -> x0, local copies, waits for them, and re-layouts: 11 us -> none  [body(): jnp.zeros((members, capacity), jnp.int32).at[target_shard, slot_rank]]
    all_to_all x1 -> x0, waiting for transfers between devices: 10.4 us -> none  [body(): lax.all_to_all(rotated_cache_pages, 'tok', split_axis=1, concat_axis=0, t...]
    all_gather x1 -> x0, waiting for transfers between devices: 10.2 us -> none  [body(): full_rows = lax.all_gather(replacement, 'head', axis=1, tiled=True)]
    unnamed x33 -> x2, local copies, waits for them, and re-layouts: 10.5 us -> 3.34 us
  transfers between devices with their start and end apart: 2 -> 0, of which waited for: 2 -> 0; matrix products, arithmetic and copies ran while one was open for 17% -> 0% of each run, Pallas kernels for 0% -> 0%
where the time goes in v1:
time: 94.8 us; the launch traced here: 94.4 us
  Pallas kernels  81.3 us (86%)
  local copies, waits for them, and re-layouts  6.69 us (7%)
  other arithmetic  5.17 us (5%)
  between operations  1.31 us (1%)
    pallas_call x1, Pallas kernels, body(): pl.pallas_call(functools.partial(kernel, members, heads, inner), out_shap...  81.3 us
    unnamed x2, local copies, waits for them, and re-layouts  3.34 us

profile of v1, /device:TPU:0, one launch (start us, length us, event | category | flops | bytes accessed | tf_op | source)
XLA Modules:
  0.0 94.4 jit_solution(9624897417954471222)
XLA Ops:
  1.3 0.7 broadcast_compare_fusion
  1.9 0.8 select_reduce_fusion.1
  2.7 1.3 %select_reduce_fusion.2 = s32[8]{0:T(128)} fusion(s32[8]{0:T(128)} %bitcast.9), kind=kLoop, calls=%fused_computation.9 | loop fusion | flops 184 | bytes 64 | tf_op jit(solution)/shard_map/reduce_sum | solution.py:334
  4.0 0.7 bitcast_add_fusion
  4.6 0.1 select_reduce_fusion
  4.8 0.7 broadcast_in_dim.81.ids_ref
  5.5 1.3 %broadcast_in_dim.74.gain_ref = bf16[1,4096]{1,0:T(2,128)(2,1)} reshape(bf16[4096]{0:T(1024)(128)(2,1)} %param.11) | data formatting | bytes 16384 | tf_op jit(solution)/shard_map/broadcast_in_dim | solution.py:390
  6.8 0.7 fusion.2.sel_ref
  7.5 1.4 %copy.13.accept_ref = s32[128,1]{1,0:T(8,128)} copy(s32[128,1]{0,1:T(1,128)} %bitcast.7) | data formatting | bytes 1024 | tf_op jit(solution)/shard_map/broadcast_in_dim | solution.py:342
  8.9 1.0 %fusion = (f32[128,128]{1,0:T(8,128)}, f32[128,128]{1,0:T(8,128)}) fusion(f32[128]{0:T(128)S(1)} %get-tuple-element.4, f32[128]{0:T(128)S(1)} %get-tuple-element.5, f32[128]{0:T(128)S(1)} %add_convert_fusion), kind=kLoop, calls=%fused_computation.2 | loop fusion | flops 32768 | bytes 132608 | tf_op jit(solution)/shard_map/mul | solution.py:331
  9.8 81.3 %shard_map.113 = (bf16[128,1024]{1,0:T(8,128)(2,1)}, bf16[128,1024]{1,0:T(8,128)(2,1)}) custom-call(s32[1,8]{1,0:T(1,128)} %bitcast.8, s32[1]{0:T(128)} %copy.16.length_ref, bf16[128,4096]{1,0:T(8,128)(2,1)} %emb_ref.1, bf16[1,4096]{1,0:T(2,128)(2,1)} %broadcast_in_dim.74.gain_ref, f32[128,128]{1,0:T(8,128)} %get-tuple-element.3.cos_ref, ...), custom_call_target="tpu_custom_call" | custom-call | tf_op jit(solution)/shard_map/pallas_call | solution.py:352
  91.1 1.7 %copy.17 = bf16[128,1024]{1,0:T(8,128)(2,1)} copy(bf16[128,1024]{1,0:T(8,128)(2,1)} %get-tuple-element.8) | data formatting | bytes 524288
  92.8 1.7 %copy.18 = bf16[128,1024]{1,0:T(8,128)(2,1)} copy(bf16[128,1024]{1,0:T(8,128)(2,1)} %get-tuple-element.9) | data formatting | bytes 524288
  (2 shorter events, 0.0 us)

commit v2 on v1

--- a/solution.py
+++ b/solution.py
@@ -21,11 +21,11 @@
 
 def kernel(
     members, heads, inner,
-    page_ref, length_ref, emb_ref, gain_ref, cos_ref, sin_ref, ids_ref, sel_ref, accept_ref,
+    owner_ref, length_ref, emb_ref, gain_ref, cos_ref, sin_ref, wanted_ref, accept_ref,
     w_hbm, table_hbm, pages_hbm,
     out1_ref, out2_ref,
     w, table, pages, x2, normed, q, kb, vb, top, total, acc,
-    ids_all, found_acc, found, recv_a, sum_a, recv_b, rows,
+    ids_ref, ids_all, found_acc, found, recv_a, sum_a, recv_b, rows,
     w_sem, table_sem, own_sem, page_send, page_recv, ids_send, ids_recv,
     a_send, a_recv, b_send, b_recv, h_send, h_recv,
 ):
@@ -45,8 +45,15 @@
     def tok_source(step):
         return lax.rem(me - step + members, members)
 
+    def crossed(step):
+        peer, bit = me, 1
+        while bit < members:
+            peer = peer + lax.rem(step // bit, 2) * bit * (1 - 2 * lax.rem(me // bit, 2))
+            bit *= 2
+        return peer
+
     def page_copy(step):
-        peer = tok_peer(step)
+        peer = crossed(step)
         return pltpu.make_async_remote_copy(
             src_ref=pages_hbm.at[0, peer], dst_ref=pages.at[me],
             send_sem=page_send.at[peer], recv_sem=page_recv.at[me],
@@ -98,12 +105,44 @@
         part = pl.ds(i * 2 * HEAD_SIZE, 2 * HEAD_SIZE)
         return pltpu.make_async_copy(w_hbm.at[:, part], w.at[:, part], w_sem.at[i])
 
+    half = members // 2
+    quarter = members // 4
+
+    def send_pages(part):
+        if part == "far0":
+            lo, hi = half, half + quarter
+        elif part == "far1":
+            lo, hi = half + quarter, members
+        elif part == "near":
+            lo, hi = 1, half
+        else:
+            lo, hi = 1, 1
+
+        @pl.loop(lo, hi)
+        def _(step):
+            page_copy(step).start()
+
     own_copy = pltpu.make_async_copy(pages_hbm.at[0, me], pages.at[me], own_sem)
 
     @pl.loop(0, table_sem.shape[0])
     def _(i):
         table_copy(i).start()
 
+    taken = accept_ref[...]
+    before_of = lax.broadcasted_iota(jnp.int32, (length, length), 0) < lax.broadcasted_iota(
+        jnp.int32, (length, length), 1
+    )
+    earlier = jnp.dot(
+        taken.astype(jnp.float32).astype(jnp.bfloat16),
+        jnp.where(before_of, 1.0, 0.0).astype(jnp.bfloat16),
+        preferred_element_type=jnp.float32,
+    ).astype(jnp.int32)
+    slot_of = lax.broadcasted_iota(jnp.int32, (slots, length), 0)
+    selected = (earlier == slot_of) & (taken == 1)
+    ids_ref[...] = jnp.broadcast_to(
+        jnp.sum(jnp.where(selected, wanted_ref[...], 0), axis=1, keepdims=True), ids_ref.shape
+    )
+
     barrier = pltpu.get_barrier_semaphore()
 
     @pl.loop(1, members)
@@ -125,9 +164,9 @@
     def _(step):
         ids_copy(tok_peer(step), me).start()
 
-    @pl.loop(1, members)
-    def _(step):
-        page_copy(step).start()
+    send_pages("far0")
+    send_pages("near")
+    send_pages("far1")
 
     for i in range(3 * groups):
         w_copy(i).start()
@@ -140,7 +179,7 @@
             part = pl.ds(pl.multiple_of(i * 16, 16), 16)
             x = x_ref[part, :].astype(jnp.float32)
             inverse = lax.rsqrt(jnp.mean(x * x, axis=-1, keepdims=True) + 1e-05)
-            normed[part, :] = (x * inverse * gain_ref[...].astype(jnp.float32)).astype(jnp.bfloat16)
+            normed[part, :] = (x * inverse * gain_ref[...].astype(jnp.float32)[None, :]).astype(jnp.bfloat16)
 
     def rotated(v):
         return (v * cos_ref[...] + pltpu.roll(v, HEAD_SIZE // 2, 1) * sin_ref[...]).astype(
@@ -186,7 +225,10 @@
             acc[p, g] = weighted(vb[p, g], e)
 
     def attend_page(source, p):
-        limit = length_ref[0] - page_ref[0, source] * page_size
+        index = jnp.int32(0)
+        for i in range(members):
+            index = index + jnp.where(owner_ref[0, i] == source, i, 0)
+        limit = length_ref[0] - index * page_size
         usable = lax.broadcasted_iota(jnp.int32, (page_size, q_rows), 0) < limit
         for g in range(groups):
             keys = pages[source, :, g * 256 : g * 256 + 128]
@@ -226,6 +268,9 @@
         a_copy(lax.rem(my_inner + step, inner), my_inner).start()
 
     project(0)
+    attend_block(0)
+    own_copy.wait()
+    attend_page(me, 0)
 
     sum_a[...] = found[:, my_inner]
 
@@ -239,8 +284,13 @@
     def _(step):
         b_copy(lax.rem(my_outer + step, outer), my_outer).start()
 
-    attend_block(0)
     rows[my_head] = sum_a[my_outer]
+
+    @pl.loop(1, half)
+    def _(step):
+        source = crossed(step)
+        page_arrival(source).wait_recv()
+        attend_page(source, 0)
 
     @pl.loop(1, outer)
     def _(step):
@@ -252,28 +302,42 @@
     def _(step):
         h_copy(lax.rem(my_head + step, heads), my_head).start()
 
-    own_copy.wait()
-    attend_page(me, 0)
+    @pl.loop(half, half + quarter)
+    def _(step):
+        source = crossed(step)
+        page_arrival(source).wait_recv()
+        attend_page(source, 0)
 
     @pl.loop(1, heads)
     def _(step):
         source = lax.rem(my_head - step + heads, heads)
         h_copy(source, source).wait_recv()
 
+    chosen = jnp.where(selected, 1.0, 0.0).astype(jnp.bfloat16)
+    replaces = lax.dot_general(
+        chosen, jnp.ones((slots, HEAD_SIZE), jnp.bfloat16), (((0,), (0,)), ((), ())),
+        preferred_element_type=jnp.float32,
+    )[:, :1] > 0.5
     for h in range(heads):
         part = slice(h * width, (h + 1) * width)
-        placed = jnp.dot(sel_ref[...], rows[h], preferred_element_type=jnp.float32)
+        placed = lax.dot_general(
+            chosen, rows[h], (((0,), (0,)), ((), ())), preferred_element_type=jnp.float32
+        )
         x2[:, part] = jnp.where(
-            accept_ref[...] == 1, placed, emb_ref[:, part].astype(jnp.float32)
+            replaces, placed, emb_ref[:, part].astype(jnp.float32)
         ).astype(jnp.bfloat16)
     normalize(x2)
     project(1)
     attend_block(1)
     attend_page(me, 1)
 
-    @pl.loop(1, members)
-    def _(step):
-        source = tok_source(step)
+    @pl.loop(1, half + quarter)
+    def _(step):
+        attend_page(crossed(step), 1)
+
+    @pl.loop(half + quarter, members)
+    def _(step):
+        source = crossed(step)
         page_arrival(source).wait_recv()
         attend_page(source, 0)
         attend_page(source, 1)
@@ -330,18 +394,7 @@
     sign = jnp.where(jnp.arange(HEAD_SIZE) < HEAD_SIZE // 2, -1.0, 1.0)
     cosine, sine = jnp.cos(turning), jnp.sin(turning) * sign[None, :]
 
-    sources = jnp.arange(members, dtype=jnp.int32)
-    page_index = jnp.sum(
-        jnp.where(page_owner_device[0][:, None] == sources[None, :], sources[:, None], 0), axis=0
-    )[None, :]
-    token_ids = vocab_shard[:, 0] * shard_rows + shard_row
-    order = jnp.arange(length)
-    earlier = jnp.sum(
-        jnp.where(order[None, :] < order[:, None], accept[None, :], 0), axis=1
-    )
-    selected = (accept[:, None] == 1) & (earlier[:, None] == jnp.arange(slots)[None, :])
-    slot_ids = jnp.sum(jnp.where(selected, token_ids[:, None], 0), axis=0)
-    slot_ids = jnp.broadcast_to(slot_ids[:, None], (slots, 128)).astype(jnp.int32)
+    token_ids = (vocab_shard[:, 0] * shard_rows + shard_row)[None, :]
 
     vmem = pl.BlockSpec(memory_space=pltpu.VMEM)
     smem = pl.BlockSpec(memory_space=pltpu.SMEM)
@@ -355,7 +408,7 @@
             jax.ShapeDtypeStruct((length, groups * q_rows), bf16),
             jax.ShapeDtypeStruct((length, groups * q_rows), bf16),
         ),
-        in_specs=[smem, smem] + [vmem] * 7 + [anywhere] * 3,
+        in_specs=[smem, smem] + [vmem] * 6 + [anywhere] * 3,
         out_specs=(vmem, vmem),
         scratch_shapes=[
             pltpu.VMEM((model, columns), bf16),
@@ -369,6 +422,7 @@
             pltpu.VMEM((2, groups, 1, q_rows), f32),
             pltpu.VMEM((2, groups, 1, q_rows), f32),
             pltpu.VMEM((2, groups, HEAD_SIZE, q_rows), f32),
+            pltpu.VMEM((slots, 128), jnp.int32),
             pltpu.VMEM((members, slots, 128), jnp.int32),
             pltpu.VMEM((members * slots, width), f32),
             pltpu.VMEM((outer, inner, slots, width), bf16),
@@ -387,8 +441,8 @@
             collective_id=0, has_side_effects=True, vmem_limit_bytes=56 * 2**20
         ),
     )(
-        page_index, cached_length, embeddings, norm_gain[None, :], cosine, sine, slot_ids,
-        selected.astype(bf16), accept[:, None],
+        page_owner_device, cached_length, embeddings, norm_gain, cosine, sine, token_ids,
+        accept[None, :],
         query_key_value_weight, embed_table, rotated_cache_pages,
     )
 

time: 94.8 us -> 85.5 us (0.902)
  local copies, waits for them, and re-layouts: 6.69 us -> 3.34 us
  other arithmetic: 5.17 us -> 2.16 us
  Pallas kernels: 81.3 us -> 78.4 us
    broadcast_in_dim x3 -> x0, local copies, waits for them, and re-layouts: 3.35 us -> none  [the longest x1 1.38 us: body(): accept[:, None] == 1]
    pallas_call x1, Pallas kernels: 81.3 us -> 78.4 us  [body(): pl.pallas_call(functools.partial(kernel, members, heads, inner), out_shap...]
    reduce_sum x3 -> x0, other arithmetic: 2.15 us -> none  [the longest x1 1.27 us: body(): jnp.sum(jnp.where(page_owner_device[0][:, None] == sources[None, :], sour...]
    broadcast_in_dim x0 -> x1, other arithmetic: none -> 1.18 us  [body(): token_ids = (vocab_shard[:, 0] * shard_rows + shard_row)[None, :]]
where the time goes in v2:
time: 85.5 us; the launch traced here: 85.2 us
  Pallas kernels  78.4 us (92%)
  local copies, waits for them, and re-layouts  3.34 us (4%)
  other arithmetic  2.16 us (3%)
  between operations  1.29 us (2%)
    pallas_call x1, Pallas kernels, body(): pl.pallas_call(functools.partial(kernel, members, heads, inner), out_shap...  78.4 us
    unnamed x2, local copies, waits for them, and re-layouts  3.34 us

profile of v2, /device:TPU:0, one launch (start us, length us, event | category | flops | bytes accessed | tf_op | source)
XLA Modules:
  0.0 85.2 jit_solution(11868059833019818897)
XLA Ops:
  1.3 1.2 %fusion.6.wanted_ref = s32[1,128]{1,0:T(1,128)} fusion(s32[128]{0:T(128)} %param.18, s32[128,1]{0,1:T(1,128)} %param.17), kind=kLoop, calls=%fused_computation.11 | loop fusion | flops 256 | bytes 1536 | tf_op jit(solution)/shard_map/broadcast_in_dim | solution.py:397
  2.5 1.0 %fusion = (f32[128,128]{1,0:T(8,128)}, f32[128,128]{1,0:T(8,128)}) fusion(f32[128]{0:T(128)S(1)} %get-tuple-element.4, f32[128]{0:T(128)S(1)} %get-tuple-element.5, f32[128]{0:T(128)S(1)} %add_convert_fusion), kind=kLoop, calls=%fused_computation.2 | loop fusion | flops 32768 | bytes 132608 | tf_op jit(solution)/shard_map/mul | solution.py:395
  3.4 78.4 %shard_map.113 = (bf16[128,1024]{1,0:T(8,128)(2,1)}, bf16[128,1024]{1,0:T(8,128)(2,1)}) custom-call(s32[1,8]{1,0:T(1,128)} %owner_ref.1, s32[1]{0:T(128)} %copy.14.length_ref, bf16[128,4096]{1,0:T(8,128)(2,1)} %emb_ref.1, bf16[4096]{0:T(1024)(128)(2,1)} %gain_ref.1, f32[128,128]{1,0:T(8,128)} %get-tuple-element.3.cos_ref, ...), custom_call_target="tpu_custom_call" | custom-call | tf_op jit(solution)/shard_map/pallas_call | solution.py:405
  81.9 1.7 %copy.15 = bf16[128,1024]{1,0:T(8,128)(2,1)} copy(bf16[128,1024]{1,0:T(8,128)(2,1)} %get-tuple-element.8) | data formatting | bytes 524288
  83.5 1.7 %copy.16 = bf16[128,1024]{1,0:T(8,128)(2,1)} copy(bf16[128,1024]{1,0:T(8,128)(2,1)} %get-tuple-element.9) | data formatting | bytes 524288
  (2 shorter events, 0.0 us)
